TPU v7x, 128 devices: a whole 4x4x4 slice. The times are simulated.
128 devices in a mesh: ex: 16 (over y, x), lay: 8 (over z, core).
Axes of the slice: x: 4, y: 4, z: 4, core: 2. Of those that a mesh axis runs over, the one named last changes fastest.
Arguments:
- grads: bfloat16 [8, 16384, 4096], P('lay', 'ex'), may hold values from -0.119628906 to 0.119628906
- prec_in: bfloat16 [8, 64, 64], P('lay'), as said below
- prec_out: bfloat16 [8, 64, 64], P('lay'), as said below
- requests: int32 [16, 16], replicated, may hold values from 0 to 7
- pairs: int32 [1024, 2], P('ex'), may hold values from 0 to 127, as said below
Outputs:
- gram: float32 [1024, 128, 128], P(('ex', 'lay'))
Inputs may be any that keep to these rules, and one draw needn't show every extreme that they name: Each device's listed first blocks are its own: pairs[p, 0] lies in 8 * (p // 64) to 8 * (p // 64 + 1) - 1. pairs[p, 1] is a device number of ex. The 64 pairs of one device are distinct and name every device number at least once. `prec_in`: each matrix has a diagonal between 1.5 and 6 and exceeds the sum of magnitudes of the rest of its row. `prec_out`: each matrix has a diagonal between 1.5 and 6 and exceeds the sum of magnitudes of the rest of its row.
All inputs are finite; a program needn't handle non-finite values.
Results may differ from a plain program's by a relative error of at most 0.0026.
Values may be sent and summed in bfloat16 or wider, within the bound.
No kernel may reach another device: no remote copies, remote signals or barrier semaphores. Data moves between devices by JAX's collectives and lax.ppermute only.
A program may use at most 128 MiB of HBM per device.

v0:
```python
import jax
import jax.numpy as jnp
from jax import lax
from jax.sharding import PartitionSpec as P

BLOCK = 128


def precondition(grads, prec_in, prec_out):
    layer_count, example_rows, width = grads.shape
    rank = prec_in.shape[-1]
    turned = jnp.swapaxes(grads, 1, 2).reshape(layer_count, rank, rank, example_rows)
    inner = jnp.einsum(
        "loie,lij->loje", turned, prec_in, preferred_element_type=jnp.float32
    ).astype(jnp.bfloat16)
    outer = jnp.einsum("lpo,loje->lpje", prec_out, inner, preferred_element_type=jnp.float32)
    return outer.astype(jnp.bfloat16).reshape(layer_count, width, example_rows)


def pick_tiles(products, first, source):
    return products[first, :, source, :]


def on_device(grads, prec_in, prec_out, requests, pairs):
    layer_count, example_rows, width = grads.shape
    blocks = grads.reshape(layer_count, example_rows // BLOCK, BLOCK, width)
    block_count = blocks.shape[1]
    member = lax.axis_index("ex")
    wanted = lax.dynamic_index_in_dim(requests, member, axis=1, keepdims=False)
    outgoing = jnp.take(blocks, wanted, axis=1)
    incoming = lax.all_to_all(outgoing, "ex", split_axis=1, concat_axis=1, tiled=True)
    holders = incoming.shape[1]
    left = precondition(grads, prec_in, prec_out)
    right = incoming.reshape(layer_count, holders * BLOCK, width)
    products = jnp.einsum("lqx,lmq->xm", left, right, preferred_element_type=jnp.float32)
    products = products.reshape(block_count, BLOCK, holders, BLOCK)
    first = pairs[:, 0] - member * block_count
    source = pairs[:, 1]
    pair_count = pairs.shape[0]
    share = pair_count // lax.axis_size("lay")
    terms = pick_tiles(products, first, source)
    total = lax.psum(terms, "lay")
    return lax.dynamic_slice_in_dim(total, lax.axis_index("lay") * share, share, 0)


def solution(mesh):
    placed = (P("lay", "ex", None), P("lay", None, None), P("lay", None, None), P(), P("ex", None))
    return jax.shard_map(
        on_device,
        mesh=mesh,
        in_specs=placed,
        out_specs=P(("ex", "lay"), None, None),
        check_vma=False,
    )
```

profile of v0, /device:TPU:0, one launch (start us, length us, event | category | flops | bytes accessed | tf_op | source)
XLA Modules:
  0.0 400.7 jit_solution(12002217262961592764)
XLA Ops:
  6.5 0.0 copy-start
  6.5 0.9 fusion.8
  7.4 0.9 and_reduce_fusion
  8.3 10.5 %gather_fusion = bf16[16,128,4096]{2,1,0:T(8,128)(2,1)} fusion(bf16[8,128,4096]{2,1,0:T(8,128)(2,1)} %bitcast.39, s32[1024]{0:T(1024)S(1)} %pad_clamp_fusion), kind=kCustom, calls=%fused_computation | custom fusion | bytes 33554496 | tf_op jit(solution)/shard_map/jit(_take)/gather | solution.py:30
  18.8 14.2 %bitcast_select_fusion = bf16[1,16,128,4096]{3,2,0,1:T(8,128)(2,1)} fusion(bf16[16,128,4096]{2,1,0:T(8,128)(2,1)} %gather_fusion, pred[16]{0:T(512)(128)(4,1)S(1)} %and_reduce_fusion), kind=kLoop, calls=%fused_computation.4 | loop fusion | flops 8388608 | bytes 33554448 | tf_op jit(solution)/shard_map/jit(_take)/select_n | solution.py:30
  33.0 7.2 %all-to-all-start = ((bf16[1,16,128,4096]{3,2,0,1:T(8,128)(2,1)}), bf16[1,16,128,4096]{3,2,0,1:T(8,128)(2,1)}, u32[]{:S(2)}, u32[]{:S(2)}) async-start(bf16[1,16,128,4096]{3,2,0,1:T(8,128)(2,1)} %bitcast_select_fusion), calls=%async_computation | async-start | bytes 33554432 | tf_op jit(solution)/shard_map/all_to_all | solution.py:31
  40.2 0.0 all-reduce.2.cloned.1.call-start
  40.3 12.0 %copy.14 = bf16[1,1024,4096]{1,2,0:T(8,128)(2,1)} copy(bf16[1,1024,4096]{2,1,0:T(8,128)(2,1)} %param.5) | data formatting | bytes 16777216 | tf_op args[0]
  52.2 0.0 copy-done
  52.2 0.0 copy-start.2
  52.2 5.8 %convert_bitcast_fusion.1 = bf16[64,64,1024]{2,1,0:T(8,128)(2,1)S(1)} fusion(bf16[64,64,1024]{2,1,0:T(8,128)(2,1)} %bitcast.40, bf16[1,64,64]{2,1,0:T(8,128)(2,1)S(1)} %copy-done), kind=kOutput, calls=%fused_computation.8 | convolution fusion | flops 541065216 | bytes 16785408 | tf_op jit(solution)/shard_map/loie,lij->loje/dot_general | solution.py:13
  58.0 0.0 copy-done.2
  58.0 12.9 %convert_bitcast_fusion = bf16[64,64,1024]{2,0,1:T(8,128)(2,1)} fusion(bf16[64,64,1024]{2,1,0:T(8,128)(2,1)S(1)} %convert_bitcast_fusion.1, bf16[1,64,64]{2,1,0:T(8,128)(2,1)S(1)} %copy-done.2), kind=kOutput, calls=%fused_computation.7 | convolution fusion | flops 541065216 | bytes 16785408 | tf_op jit(solution)/shard_map/lpo,loje->lpje/dot_general | solution.py:16
  70.9 11.3 %copy.17 = bf16[64,64,1024]{2,1,0:T(8,128)(2,1)} copy(bf16[64,64,1024]{2,0,1:T(8,128)(2,1)} %convert_bitcast_fusion) | data formatting | bytes 16777216 | tf_op jit(solution)/shard_map/convert_element_type | solution.py:17
  82.2 11.2 %copy.22 = bf16[1024,4096]{1,0:T(8,128)(2,1)} copy(bf16[1024,4096]{0,1:T(8,128)(2,1)} %bitcast.41) | data formatting | bytes 16777216 | tf_op jit(solution)/shard_map/lqx,lmq->xm/dot_general | solution.py:35
  93.4 0.0 copy-done.3
  93.4 196.5 %all-to-all-done = bf16[1,16,128,4096]{3,2,0,1:T(8,128)(2,1)} async-done(((bf16[1,16,128,4096]{3,2,0,1:T(8,128)(2,1)}), bf16[1,16,128,4096]{3,2,0,1:T(8,128)(2,1)}, u32[]{:S(2)}, u32[]{:S(2)}) %all-to-all-start) | async-done | bytes 16777248 | tf_op jit(solution)/shard_map/all_to_all | solution.py:31
  289.9 0.0 copy-start.1
  289.9 24.1 %fusion = f32[8,128,16,128]{3,1,2,0:T(8,128)} fusion(bf16[8,128,4096,1]{2,1,3,0:T(8,128)(2,1)} %bitcast.42, bf16[1,16,128,4096]{3,2,0,1:T(8,128)(2,1)} %all-to-all-done), kind=kOutput, calls=%fused_computation.2 | convolution fusion | flops 17179869184 | bytes 33554432 | tf_op jit(solution)/shard_map/lqx,lmq->xm/dot_general | solution.py:35
  314.0 6.1 %gather_fusion.1 = f32[64,128,128]{2,1,0:T(8,128)} fusion(f32[8,128,16,128]{3,1,2,0:T(8,128)} %fusion, s32[64]{0:T(128)S(1)} %fusion.14), kind=kCustom, calls=%fused_computation.1 | custom fusion | bytes 8389120 | tf_op jit(solution)/shard_map/gather | solution.py:21
  320.2 0.0 all-reduce.2.cloned.1.call-update
  320.2 71.8 %all-reduce.2.cloned.1.call-done = f32[64,128,128]{2,1,0:T(8,128)} async-done(((f32[64,128,128]{2,1,0:T(8,128)}), f32[64,128,128]{2,1,0:T(8,128)}) %all-reduce.2.cloned.1.call-update) | async-done | bytes 4194320 | tf_op jit(solution)/shard_map/psum | solution.py:42
  392.0 1.9 constant_dynamic-slice_fusion
  393.9 0.0 copy-done.1
  (3 shorter events, 0.0 us)
Async XLA Ops:
  6.5 45.7 %copy-start = (bf16[1,64,64]{2,1,0:T(8,128)(2,1)S(1)}, bf16[1,64,64]{2,1,0:T(8,128)(2,1)}, u32[]{:S(2)}) copy-start(bf16[1,64,64]{2,1,0:T(8,128)(2,1)} %param.6) | copy-start | bytes 24580
  33.0 257.0 %all-to-all-start = ((bf16[1,16,128,4096]{3,2,0,1:T(8,128)(2,1)}), bf16[1,16,128,4096]{3,2,0,1:T(8,128)(2,1)}, u32[]{:S(2)}, u32[]{:S(2)}) async-start(bf16[1,16,128,4096]{3,2,0,1:T(8,128)(2,1)} %bitcast_select_fusion), calls=%async_computation | async-start | bytes 33554432 | tf_op jit(solution)/shard_map/all_to_all | solution.py:31
  40.2 351.8 %all-reduce.2.cloned.1.call-start = ((), (), s32[]{:S(2)}) async-start(), calls=%async_computation.1 | async-start | bytes 8388608 | tf_op jit(solution)/shard_map/psum | solution.py:42
  52.2 5.8 %copy-start.2 = (bf16[1,64,64]{2,1,0:T(8,128)(2,1)S(1)}, bf16[1,64,64]{2,1,0:T(8,128)(2,1)}, u32[]{:S(2)}) copy-start(bf16[1,64,64]{2,1,0:T(8,128)(2,1)} %param.7) | copy-start | bytes 24580
  82.2 11.2 %copy-start.3 = (s32[64,2]{0,1:T(2,128)S(1)}, s32[64,2]{0,1:T(2,128)}, u32[]{:S(2)}) copy-start(s32[64,2]{0,1:T(2,128)} %param.9) | copy-start | bytes 1540
  289.9 103.9 %copy-start.1 = (bf16[1,64,64]{2,1,0:T(8,128)(2,1)S(1)}, bf16[1,64,64]{2,1,0:T(8,128)(2,1)}, u32[]{:S(2)}) copy-start(bf16[1,64,64]{2,1,0:T(8,128)(2,1)} %param.6) | copy-start | bytes 24580
Sparse Core Ops, SparseCore 0:
  320.3 71.6 all-reduce.1
where the time goes:
time: 402 us; the launch traced here: 401 us
  waiting for transfers between devices  268 us (67%)
  local copies, waits for them, and re-layouts  53 us (13%)
  matrix products  42.8 us (11%)
  other arithmetic  15.9 us (4%)
  between operations  13.4 us (3%)
  starting transfers between devices  7.28 us (2%)
    all_to_all x1, waiting for transfers between devices, on_device(): lax.all_to_all(outgoing, 'ex', split_axis=1, concat_axis=1, tiled=True)  197 us
    psum x1, waiting for transfers between devices, on_device(): total = lax.psum(terms, 'lay')  71.8 us
    dot_general x1, matrix products, on_device(): jnp.einsum('lqx,lmq->xm', left, right, preferred_element_type=jnp.float32)  24.1 us
    select_n x2, other arithmetic, on_device(): outgoing = jnp.take(blocks, wanted, axis=1)  15 us
    dot_general x1, matrix products, precondition(): jnp.einsum('lpo,loje->lpje', prec_out, inner, preferred_element_type=jnp....  12.9 us
    unnamed x9, local copies, waits for them, and re-layouts  12 us
    convert_element_type x1, local copies, waits for them, and re-layouts, precondition(): return outer.astype(jnp.bfloat16).reshape(layer_count, width, example_rows)  11.3 us
    dot_general x1, local copies, waits for them, and re-layouts, on_device(): jnp.einsum('lqx,lmq->xm', left, right, preferred_element_type=jnp.float32)  11.2 us
  transfers between devices with their start and end apart: 2, of which 2 were waited for; matrix products, arithmetic and copies ran while one was open for 13% of the time, Pallas kernels for 0%

commit v1 on v0

--- a/solution.py
+++ b/solution.py
@@ -39,7 +39,9 @@
     pair_count = pairs.shape[0]
     share = pair_count // lax.axis_size("lay")
     terms = pick_tiles(products, first, source)
-    total = lax.psum(terms, "lay")
+    total = terms
+    for hop in (1, 2, 4):
+        total = total + lax.ppermute(total, "lay", [(dev, dev ^ hop) for dev in range(8)])
     return lax.dynamic_slice_in_dim(total, lax.axis_index("lay") * share, share, 0)
 
 

time: 402 us -> 517 us (1.29)
  waiting for transfers between devices: 268 us -> 385 us
  between operations: 13.4 us -> 0.05 us
  other arithmetic: 15.9 us -> 23.7 us
  starting transfers between devices: 7.28 us -> 12.9 us
    ppermute x0 -> x3, waiting for transfers between devices: none -> 189 us  [on_device(): lax.ppermute(total, 'lay', [(dev, dev ^ hop) for dev in range(8)])]
    psum x1 -> x0, waiting for transfers between devices: 71.8 us -> none  [on_device(): total = lax.psum(terms, 'lay')]
    add x0 -> x3, other arithmetic: none -> 7.71 us  [on_device(): total + lax.ppermute(total, 'lay', [(dev, dev ^ hop) for dev in range(8)])]
    ppermute x0 -> x3, starting transfers between devices: none -> 5.7 us  [on_device(): lax.ppermute(total, 'lay', [(dev, dev ^ hop) for dev in range(8)])]
  transfers between devices with their start and end apart: 2 -> 4, of which waited for: 2 -> 4; matrix products, arithmetic and copies ran while one was open for 13% -> 10% of each run, Pallas kernels for 0% -> 0%
where the time goes in v1:
time: 517 us; the launch traced here: 516 us
  waiting for transfers between devices  385 us (74%)
  local copies, waits for them, and re-layouts  51.3 us (10%)
  matrix products  42.8 us (8%)
  other arithmetic  23.7 us (5%)
  starting transfers between devices  12.9 us (2%)
    all_to_all x1, waiting for transfers between devices, on_device(): lax.all_to_all(outgoing, 'ex', split_axis=1, concat_axis=1, tiled=True)  196 us
    ppermute x3, waiting for transfers between devices, on_device(): lax.ppermute(total, 'lay', [(dev, dev ^ hop) for dev in range(8)])  189 us
    dot_general x1, matrix products, on_device(): jnp.einsum('lqx,lmq->xm', left, right, preferred_element_type=jnp.float32)  24.1 us
    select_n x2, other arithmetic, on_device(): outgoing = jnp.take(blocks, wanted, axis=1)  15 us
    dot_general x1, matrix products, precondition(): jnp.einsum('lpo,loje->lpje', prec_out, inner, preferred_element_type=jnp....  12.9 us
    unnamed x9, local copies, waits for them, and re-layouts  12 us
    dot_general x1, local copies, waits for them, and re-layouts, on_device(): jnp.einsum('lqx,lmq->xm', left, right, preferred_element_type=jnp.float32)  11.4 us
    convert_element_type x1, local copies, waits for them, and re-layouts, precondition(): return outer.astype(jnp.bfloat16).reshape(layer_count, width, example_rows)  11.3 us
  transfers between devices with their start and end apart: 4, of which 4 were waited for; matrix products, arithmetic and copies ran while one was open for 10% of the time, Pallas kernels for 0%

profile of v1, /device:TPU:0, one launch (start us, length us, event | category | flops | bytes accessed | tf_op | source)
XLA Modules:
  0.0 515.7 jit_solution(11605448485297509987)
XLA Ops:
  0.0 0.0 copy-start
  0.0 0.9 fusion.8
  0.9 0.9 and_reduce_fusion
  1.8 10.5 %gather_fusion = bf16[16,128,4096]{2,1,0:T(8,128)(2,1)} fusion(bf16[8,128,4096]{2,1,0:T(8,128)(2,1)} %bitcast.39, s32[1024]{0:T(1024)S(1)} %pad_clamp_fusion), kind=kCustom, calls=%fused_computation | custom fusion | bytes 33554496 | tf_op jit(solution)/shard_map/jit(_take)/gather | solution.py:30
  12.3 14.2 %bitcast_select_fusion = bf16[1,16,128,4096]{3,2,0,1:T(8,128)(2,1)} fusion(bf16[16,128,4096]{2,1,0:T(8,128)(2,1)} %gather_fusion, pred[16]{0:T(512)(128)(4,1)S(1)} %and_reduce_fusion), kind=kLoop, calls=%fused_computation.4 | loop fusion | flops 8388608 | bytes 33554448 | tf_op jit(solution)/shard_map/jit(_take)/select_n | solution.py:30
  26.4 7.2 %all-to-all-start = ((bf16[1,16,128,4096]{3,2,0,1:T(8,128)(2,1)}), bf16[1,16,128,4096]{3,2,0,1:T(8,128)(2,1)}, u32[]{:S(2)}, u32[]{:S(2)}) async-start(bf16[1,16,128,4096]{3,2,0,1:T(8,128)(2,1)} %bitcast_select_fusion), calls=%async_computation | async-start | bytes 33554432 | tf_op jit(solution)/shard_map/all_to_all | solution.py:31
  33.7 12.0 %copy.14 = bf16[1,1024,4096]{1,2,0:T(8,128)(2,1)} copy(bf16[1,1024,4096]{2,1,0:T(8,128)(2,1)} %param.5) | data formatting | bytes 16777216 | tf_op args[0]
  45.7 0.0 copy-done
  45.7 5.8 %convert_bitcast_fusion.1 = bf16[64,64,1024]{2,1,0:T(8,128)(2,1)S(1)} fusion(bf16[64,64,1024]{2,1,0:T(8,128)(2,1)} %bitcast.40, bf16[1,64,64]{2,1,0:T(8,128)(2,1)S(1)} %copy-done), kind=kOutput, calls=%fused_computation.8 | convolution fusion | flops 541065216 | bytes 16785408 | tf_op jit(solution)/shard_map/loie,lij->loje/dot_general | solution.py:13
  51.4 12.9 %convert_bitcast_fusion = bf16[64,64,1024]{2,0,1:T(8,128)(2,1)} fusion(bf16[64,64,1024]{2,1,0:T(8,128)(2,1)S(1)} %convert_bitcast_fusion.1, bf16[1,64,64]{2,1,0:T(8,128)(2,1)S(1)} %copy-done.2), kind=kOutput, calls=%fused_computation.7 | convolution fusion | flops 541065216 | bytes 16785408 | tf_op jit(solution)/shard_map/lpo,loje->lpje/dot_general | solution.py:16
  64.3 11.3 %copy.17 = bf16[64,64,1024]{2,1,0:T(8,128)(2,1)} copy(bf16[64,64,1024]{2,0,1:T(8,128)(2,1)} %convert_bitcast_fusion) | data formatting | bytes 16777216 | tf_op jit(solution)/shard_map/convert_element_type | solution.py:17
  75.6 11.4 %copy.22 = bf16[1024,4096]{1,0:T(8,128)(2,1)} copy(bf16[1024,4096]{0,1:T(8,128)(2,1)} %bitcast.41) | data formatting | bytes 16777216 | tf_op jit(solution)/shard_map/lqx,lmq->xm/dot_general | solution.py:35
  87.1 196.3 %all-to-all-done = bf16[1,16,128,4096]{3,2,0,1:T(8,128)(2,1)} async-done(((bf16[1,16,128,4096]{3,2,0,1:T(8,128)(2,1)}), bf16[1,16,128,4096]{3,2,0,1:T(8,128)(2,1)}, u32[]{:S(2)}, u32[]{:S(2)}) %all-to-all-start) | async-done | bytes 16777248 | tf_op jit(solution)/shard_map/all_to_all | solution.py:31
  283.4 24.1 %fusion = f32[8,128,16,128]{3,1,2,0:T(8,128)} fusion(bf16[8,128,4096,1]{2,1,3,0:T(8,128)(2,1)} %bitcast.42, bf16[1,16,128,4096]{3,2,0,1:T(8,128)(2,1)} %all-to-all-done), kind=kOutput, calls=%fused_computation.2 | convolution fusion | flops 17179869184 | bytes 33554432 | tf_op jit(solution)/shard_map/lqx,lmq->xm/dot_general | solution.py:35
  307.5 6.1 %gather_fusion.1 = f32[64,128,128]{2,1,0:T(8,128)} fusion(f32[8,128,16,128]{3,1,2,0:T(8,128)} %fusion, s32[64]{0:T(128)S(1)} %fusion.14), kind=kCustom, calls=%fused_computation.1 | custom fusion | bytes 8389120 | tf_op jit(solution)/shard_map/gather | solution.py:21
  313.7 0.0 collective-permute-start
  313.7 7.4 %collective-permute-done = f32[64,128,128]{2,1,0:T(8,128)S(1)} collective-permute-done((f32[64,128,128]{2,1,0:T(8,128)}, f32[64,128,128]{2,1,0:T(8,128)S(1)}, u32[]{:S(2)}, u32[]{:S(2)}) %collective-permute-start) | collective-permute-done | bytes 4194336 | tf_op jit(solution)/shard_map/ppermute | solution.py:44
  321.0 3.0 add.42
  324.0 2.0 collective-permute-start.1
  326.0 90.9 %collective-permute-done.1 = f32[64,128,128]{2,1,0:T(8,128)S(1)} collective-permute-done((f32[64,128,128]{2,1,0:T(8,128)S(1)}, f32[64,128,128]{2,1,0:T(8,128)S(1)}, u32[]{:S(2)}, u32[]{:S(2)}) %collective-permute-start.1) | collective-permute-done | bytes 4194336 | tf_op jit(solution)/shard_map/ppermute | solution.py:44
  416.9 2.7 add.43
  419.6 3.7 collective-permute-start.2
  423.3 90.4 %collective-permute-done.2 = f32[64,128,128]{2,1,0:T(8,128)} collective-permute-done((f32[64,128,128]{2,1,0:T(8,128)}, f32[64,128,128]{2,1,0:T(8,128)}, u32[]{:S(2)}, u32[]{:S(2)}) %collective-permute-start.2) | collective-permute-done | bytes 4194336 | tf_op jit(solution)/shard_map/ppermute | solution.py:44
  513.6 2.0 dynamic-slice_add_fusion
  (8 shorter events, 0.0 us)
Async XLA Ops:
  0.0 45.7 %copy-start = (bf16[1,64,64]{2,1,0:T(8,128)(2,1)S(1)}, bf16[1,64,64]{2,1,0:T(8,128)(2,1)}, u32[]{:S(2)}) copy-start(bf16[1,64,64]{2,1,0:T(8,128)(2,1)} %param.6) | copy-start | bytes 24580
  26.4 257.0 %all-to-all-start = ((bf16[1,16,128,4096]{3,2,0,1:T(8,128)(2,1)}), bf16[1,16,128,4096]{3,2,0,1:T(8,128)(2,1)}, u32[]{:S(2)}, u32[]{:S(2)}) async-start(bf16[1,16,128,4096]{3,2,0,1:T(8,128)(2,1)} %bitcast_select_fusion), calls=%async_computation | async-start | bytes 33554432 | tf_op jit(solution)/shard_map/all_to_all | solution.py:31
  45.7 5.8 %copy-start.2 = (bf16[1,64,64]{2,1,0:T(8,128)(2,1)S(1)}, bf16[1,64,64]{2,1,0:T(8,128)(2,1)}, u32[]{:S(2)}) copy-start(bf16[1,64,64]{2,1,0:T(8,128)(2,1)} %param.7) | copy-start | bytes 24580
  75.6 11.5 %copy-start.3 = (s32[64,2]{0,1:T(2,128)S(1)}, s32[64,2]{0,1:T(2,128)}, u32[]{:S(2)}) copy-start(s32[64,2]{0,1:T(2,128)} %param.9) | copy-start | bytes 1540
  313.7 7.4 %collective-permute-start = (f32[64,128,128]{2,1,0:T(8,128)}, f32[64,128,128]{2,1,0:T(8,128)S(1)}, u32[]{:S(2)}, u32[]{:S(2)}) collective-permute-start(f32[64,128,128]{2,1,0:T(8,128)} %gather_fusion.1), channel_id=1, source_target_pairs={{0,1},{1,0},{2,3},{3,2},{4,5},{5,4},{6,7},{7,6},{8,9},{9,8},{10,11... | collective-permute-start | bytes 12582920 | tf_op jit(solution)/shard_map/ppermute | solution.py:44
  321.0 194.6 %copy-start.1 = (bf16[1,64,64]{2,1,0:T(8,128)(2,1)S(1)}, bf16[1,64,64]{2,1,0:T(8,128)(2,1)}, u32[]{:S(2)}) copy-start(bf16[1,64,64]{2,1,0:T(8,128)(2,1)} %param.6) | copy-start | bytes 24580
  324.0 92.9 %collective-permute-start.1 = (f32[64,128,128]{2,1,0:T(8,128)S(1)}, f32[64,128,128]{2,1,0:T(8,128)S(1)}, u32[]{:S(2)}, u32[]{:S(2)}) collective-permute-start(f32[64,128,128]{2,1,0:T(8,128)S(1)} %add.42), channel_id=1, source_target_pairs={{0,2},{1,3},{2,0},{3,1},{4,6},{5,7},{6,4},{7,5},{8,10},{9,11},{10,... | collective-permute-start | bytes 12582920 | tf_op jit(solution)/shard_map/ppermute | solution.py:44
  419.6 94.1 %collective-permute-start.2 = (f32[64,128,128]{2,1,0:T(8,128)}, f32[64,128,128]{2,1,0:T(8,128)}, u32[]{:S(2)}, u32[]{:S(2)}) collective-permute-start(f32[64,128,128]{2,1,0:T(8,128)} %add.43), channel_id=1, source_target_pairs={{0,4},{1,5},{2,6},{3,7},{4,0},{5,1},{6,2},{7,3},{8,12},{9,13},{10,... | collective-permute-start | bytes 12582920 | tf_op jit(solution)/shard_map/ppermute | solution.py:44
